TPU v7x, 32 devices: a whole 2x2x4 slice. The times are simulated.
32 devices in a mesh: entry: 4 (over y, core), fft: 8 (over z, x).
Axes of the slice: x: 2, y: 2, z: 4, core: 2. Of those that a mesh axis runs over, the one named last changes fastest.
Arguments:
- left_zero_zero: int32 [2048, 4096], P('entry', 'fft'), may hold values from 0 to 65535
- left_zero_one: int32 [2048, 4096], P('entry', 'fft'), may hold values from 0 to 65535
- left_one_zero: int32 [2048, 4096], P('entry', 'fft'), may hold values from 0 to 65535
- left_one_one: int32 [2048, 4096], P('entry', 'fft'), may hold values from 0 to 65535
- right_zero_zero: int32 [2048, 4096], P('entry', 'fft'), may hold values from 0 to 65535
- right_zero_one: int32 [2048, 4096], P('entry', 'fft'), may hold values from 0 to 65535
- right_one_zero: int32 [2048, 4096], P('entry', 'fft'), may hold values from 0 to 65535
- right_one_one: int32 [2048, 4096], P('entry', 'fft'), may hold values from 0 to 65535
Outputs:
- product: float32 [4, 4096, 4096], P('entry', None, 'fft')
All inputs are finite; a program needn't handle non-finite values.
Results may differ from a plain program's by a relative error of at most 0.0001.
Values sent between devices are 32-bit elements; how exact they have to be, the bound alone decides.
A program may use at most 384 MiB of HBM per device.

v0:
```python
import math

import jax
import jax.numpy as jnp
from jax import lax
from jax.sharding import PartitionSpec as P

RADIX = 64


exact_precision = lax.Precision.HIGHEST


def matmul(left_op, right_op):
    return jnp.dot(left_op, right_op, precision=exact_precision, preferred_element_type=jnp.float32)


def contract(pattern, left_op, right_op):
    return jnp.einsum(
        pattern, left_op, right_op, precision=exact_precision, preferred_element_type=jnp.float32
    )


def angle_table(first_part, second_part, length, sense_sign):
    turns = first_part[:, None] * second_part[None, :] % length
    phase_angle = turns.astype(jnp.float32) * (2.0 * math.pi / length)
    return (jnp.cos(phase_angle), sense_sign * jnp.sin(phase_angle))


def rotate(real_part, imag_part, cosine, sine):
    return (real_part * cosine - imag_part * sine, real_part * sine + imag_part * cosine)


def complex_product(left_real, left_imag, right_real, right_imag):
    return (
        left_real * right_real - left_imag * right_imag,
        left_real * right_imag + left_imag * right_real,
    )


def digits(limbs):
    return (limbs.astype(jnp.float32) - 32768.0) * (1.0 / 32768.0)


def column_transform(real_part, imag_part, length, radix_size, sense_sign, real_only):
    inner_size = length // radix_size
    outer_count = real_part.shape[0] // inner_size
    column_count = real_part.shape[1]
    first_cos, first_sin = angle_table(
        jnp.arange(radix_size, dtype=jnp.int32),
        jnp.arange(outer_count, dtype=jnp.int32),
        radix_size,
        sense_sign,
    )
    flat_real = real_part.reshape(outer_count, inner_size * column_count)
    step_real = matmul(first_cos, flat_real)
    step_imag = matmul(first_sin, flat_real)
    if imag_part is not None:
        flat_imag = imag_part.reshape(outer_count, inner_size * column_count)
        step_real = step_real - matmul(first_sin, flat_imag)
        step_imag = step_imag + matmul(first_cos, flat_imag)
    step_real = step_real.reshape(radix_size, inner_size, column_count)
    step_imag = step_imag.reshape(radix_size, inner_size, column_count)
    twist_cos, twist_sin = angle_table(
        jnp.arange(radix_size, dtype=jnp.int32),
        jnp.arange(inner_size, dtype=jnp.int32),
        length,
        sense_sign,
    )
    step_real, step_imag = rotate(
        step_real, step_imag, twist_cos[:, :, None], twist_sin[:, :, None]
    )
    second_cos, second_sin = angle_table(
        jnp.arange(inner_size, dtype=jnp.int32),
        jnp.arange(inner_size, dtype=jnp.int32),
        inner_size,
        sense_sign,
    )
    final_real = contract("mb,kbc->mkc", second_cos, step_real) - contract(
        "mb,kbc->mkc", second_sin, step_imag
    )
    final_real = final_real.reshape(length, column_count)
    if real_only:
        return final_real
    final_imag = contract("mb,kbc->mkc", second_sin, step_real) + contract(
        "mb,kbc->mkc", second_cos, step_imag
    )
    return (final_real, final_imag.reshape(length, column_count))


def row_transform(real_part, imag_part, length, radix_size, sense_sign):
    inner_size = length // radix_size
    row_count = real_part.shape[0]
    shaped_real = real_part.reshape(row_count, radix_size, inner_size)
    shaped_imag = imag_part.reshape(row_count, radix_size, inner_size)
    first_cos, first_sin = angle_table(
        jnp.arange(radix_size, dtype=jnp.int32),
        jnp.arange(radix_size, dtype=jnp.int32),
        radix_size,
        sense_sign,
    )
    step_real = contract("rab,ak->rkb", shaped_real, first_cos) - contract(
        "rab,ak->rkb", shaped_imag, first_sin
    )
    step_imag = contract("rab,ak->rkb", shaped_real, first_sin) + contract(
        "rab,ak->rkb", shaped_imag, first_cos
    )
    twist_cos, twist_sin = angle_table(
        jnp.arange(radix_size, dtype=jnp.int32),
        jnp.arange(inner_size, dtype=jnp.int32),
        length,
        sense_sign,
    )
    step_real, step_imag = rotate(step_real, step_imag, twist_cos[None], twist_sin[None])
    second_cos, second_sin = angle_table(
        jnp.arange(inner_size, dtype=jnp.int32),
        jnp.arange(inner_size, dtype=jnp.int32),
        inner_size,
        sense_sign,
    )
    final_real = contract("rkb,bm->rmk", step_real, second_cos) - contract(
        "rkb,bm->rmk", step_imag, second_sin
    )
    final_imag = contract("rkb,bm->rmk", step_real, second_sin) + contract(
        "rkb,bm->rmk", step_imag, second_cos
    )
    return (final_real.reshape(row_count, length), final_imag.reshape(row_count, length))


def local(
    left_zero_zero,
    left_zero_one,
    left_one_zero,
    left_one_one,
    right_zero_zero,
    right_zero_one,
    right_one_zero,
    right_one_one,
):
    lefts = [
        [digits(left_zero_zero), digits(left_zero_one)],
        [digits(left_one_zero), digits(left_one_one)],
    ]
    rights = [
        [digits(right_zero_zero), digits(right_zero_one)],
        [digits(right_one_zero), digits(right_one_one)],
    ]
    chosen = [
        [lefts[target // 2][0], lefts[target // 2][1], rights[0][target % 2], rights[1][target % 2]]
        for target in range(4)
    ]
    outgoing = jnp.stack([jnp.stack(member_list) for member_list in chosen], axis=1)
    arrived = lax.all_to_all(outgoing, "entry", split_axis=1, concat_axis=1, tiled=True)
    member_count = arrived.shape[0]
    local_cols = arrived.shape[3]
    arrived = arrived.reshape(member_count, -1, local_cols)
    row_count = 2 * arrived.shape[1]
    column_count = local_cols * lax.axis_size("fft")
    length = row_count * column_count
    fft_place = lax.axis_index("fft")
    global_cols = fft_place * local_cols + jnp.arange(local_cols, dtype=jnp.int32)
    twist_cos, twist_sin = angle_table(
        jnp.arange(row_count, dtype=jnp.int32), global_cols, length, -1.0
    )
    real_list = []
    imag_list = []
    for member in range(member_count):
        part_real, part_imag = column_transform(
            arrived[member], None, row_count, RADIX, -1.0, False
        )
        part_real, part_imag = rotate(part_real, part_imag, twist_cos, twist_sin)
        real_list.append(part_real)
        imag_list.append(part_imag)
    piece_real = lax.all_to_all(
        jnp.stack(real_list), "fft", split_axis=1, concat_axis=2, tiled=True
    )
    piece_imag = lax.all_to_all(
        jnp.stack(imag_list), "fft", split_axis=1, concat_axis=2, tiled=True
    )
    done_real = []
    done_imag = []
    for member in range(piece_real.shape[0]):
        out_real, out_imag = row_transform(
            piece_real[member], piece_imag[member], column_count, RADIX, -1.0
        )
        done_real.append(out_real)
        done_imag.append(out_imag)
    spec_real = jnp.stack(done_real)
    spec_imag = jnp.stack(done_imag)
    head_real, head_imag = complex_product(spec_real[0], spec_imag[0], spec_real[2], spec_imag[2])
    rest_real, rest_imag = complex_product(spec_real[1], spec_imag[1], spec_real[3], spec_imag[3])
    mixed_real = head_real + rest_real
    mixed_imag = head_imag + rest_imag
    mixed_real, mixed_imag = row_transform(mixed_real, mixed_imag, column_count, RADIX, 1.0)
    local_rows = mixed_real.shape[0]
    row_ids = fft_place * local_rows + jnp.arange(local_rows, dtype=jnp.int32)
    back_cos, back_sin = angle_table(
        row_ids, jnp.arange(column_count, dtype=jnp.int32), length, 1.0
    )
    mixed_real, mixed_imag = rotate(mixed_real, mixed_imag, back_cos, back_sin)
    full_real, full_imag = (
        lax.all_to_all(mixed_real, "fft", split_axis=1, concat_axis=0, tiled=True),
        lax.all_to_all(mixed_imag, "fft", split_axis=1, concat_axis=0, tiled=True),
    )
    values = column_transform(full_real, full_imag, row_count, RADIX, 1.0, True)
    out_scale = 1.0 / (length * math.sqrt(length // 2))
    return (values * out_scale)[None]


def solution(mesh):
    placed = (
        P("entry", "fft"),
        P("entry", "fft"),
        P("entry", "fft"),
        P("entry", "fft"),
        P("entry", "fft"),
        P("entry", "fft"),
        P("entry", "fft"),
        P("entry", "fft"),
    )
    return jax.shard_map(
        local, mesh=mesh, in_specs=placed, out_specs=P("entry", None, "fft"), check_vma=False
    )
```

profile of v0, /device:TPU:0, one launch (start us, length us, event | category | flops | bytes accessed | tf_op | source)
XLA Modules:
  0.0 3396.6 jit_solution(7557897926247349218)
XLA Ops:
  21.3 182.6 %all-to-all-done = f32[4,4,512,512]{3,2,0,1:T(8,128)} async-done(((f32[4,4,512,512]{3,2,0,1:T(8,128)}), f32[4,4,512,512]{3,2,0,1:T(8,128)}, u32[]{:S(2)}, u32[]{:S(2)}) %all-to-all-start) | async-done | bytes 16777248 | tf_op jit(solution)/shard_map/all_to_all | solution.py:153
  307.5 45.5 %multiply_subtract_fusion.3 = (f32[64,64,512]{2,0,1:T(8,128)}, f32[64,64,512]{2,0,1:T(8,128)}, f32[64,64,512]{2,0,1:T(8,128)}, f32[64,64,512]{2,0,1:T(8,128)}, f...) fusion(f32[64,64,512]{2,0,1:T(8,128)} %fusion.155, ...), kind=kOutput, calls=%fused_computation.92 | convolution fusion | flops 855668736 | bytes 130056192 | tf_op jit(solution)/shard_map/dot_general | solution.py:15
  353.0 18.2 fusion.107
  424.5 13.6 fusion.121
  464.8 13.8 fusion.186
  490.4 16.1 fusion.189
  518.0 15.2 fusion.180
  541.3 15.7 fusion.183
  568.7 15.9 fusion.174
  596.3 15.7 fusion.177
  623.6 15.2 fusion.168
  647.0 15.9 fusion.171
  674.7 46.0 %fusion.25 = (f32[1,4096,512]{2,1,0:T(8,128)}, f32[1,4096,512]{2,1,0:T(8,128)}, f32[1,4096,512]{2,1,0:T(8,128)}, f32[1,4096,512]{2,1,0:T(8,128)}, f32[1,4096,512...) fusion(s32[512]{0:T(512)S(1)} %copy-done.25, ...), kind=kLoop, calls=%fused_computation.60 | loop fusion | flops 81788928 | bytes 134219776 | tf_op jit(solution)/shard_map/add | solution.py:31
  720.7 22.9 pad_maximum_fusion.1
  743.6 37.9 %copy.386 = f32[4,4096,512]{2,0,1:T(4,128)} copy(f32[4,4096,512]{2,1,0:T(8,128)} %pad_maximum_fusion.1) | data formatting | bytes 67108864 | tf_op jit(solution)/shard_map/stack | solution.py:178
  788.9 22.9 pad_maximum_fusion
  811.8 37.9 %copy.381 = f32[4,4096,512]{2,0,1:T(4,128)} copy(f32[4,4096,512]{2,1,0:T(8,128)} %pad_maximum_fusion) | data formatting | bytes 67108864 | tf_op jit(solution)/shard_map/stack | solution.py:175
  849.8 663.8 %all-to-all-done.2 = f32[4,4096,512]{2,0,1:T(4,128)} async-done(((f32[4,4096,512]{2,0,1:T(4,128)}), f32[4,4096,512]{2,0,1:T(4,128)}, u32[]{:S(2)}, u32[]{:S(2)}) %all-to-all-start.2) | async-done | bytes 33554464 | tf_op jit(solution)/shard_map/all_to_all | solution.py:177
  1522.1 30.6 copy.387
  1552.7 24.3 fusion.646
  1613.5 18.1 fusion.49
  1631.5 18.0 fusion.51
  1649.6 13.9 fusion.65
  1730.4 512.2 %all-to-all-done.1 = f32[4,4096,512]{2,0,1:T(4,128)} async-done(((f32[4,4096,512]{2,0,1:T(4,128)}), f32[4,4096,512]{2,0,1:T(4,128)}, u32[]{:S(2)}, u32[]{:S(2)}) %all-to-all-start.1) | async-done | bytes 33554464 | tf_op jit(solution)/shard_map/all_to_all | solution.py:174
  2242.6 31.0 copy.382
  2273.6 24.3 fusion.647
  2307.0 17.9 fusion.53
  2347.4 18.0 fusion.69
  2365.4 13.6 fusion.71
  2388.1 18.0 fusion.85
  2406.1 13.9 fusion.87
  2429.1 17.8 fusion.101
  2446.9 64.3 %add_bitcast_fusion.5 = (f32[512,64,64]{0,1,2:T(8,128)}, f32[512,64,64]{0,1,2:T(8,128)}, f32[512,64,64]{0,1,2:T(8,128)}, f32[512,64,64]{0,1,2:T(8,128)}, f32[512...) fusion(f32[64,64]{0,1:T(8,128)S(1)} %copy-done.22, ...), kind=kOutput, calls=%fused_computation.80 | convolution fusion | flops 1677778944 | bytes 201359360 | tf_op jit(solution)/shard_map/rab,ak->rkb/dot_general | solution.py:19
  2511.2 18.0 fusion.41
  2529.3 13.8 fusion.43
  2556.4 13.5 fusion.59
  2583.1 13.5 fusion.63
  2609.9 13.7 fusion.75
  2690.7 13.7 fusion.95
  2717.7 51.4 %add_add_fusion = (f32[64,512,64]{1,0,2:T(8,128)}, f32[64,512,64]{1,0,2:T(8,128)}) fusion(f32[64,512,64]{1,0,2:T(8,128)} %fusion.41, f32[64,512,64]{1,0,2:T(8,128)} %fusion.61, f32[64,512,64]{1,0,2:T(8,128)} %fusion.57, f32[64,512,64]{1,0,2:T(8,128)} %fusion.47, f32[64,512,64]{1,0,2:T(8,128)} %fusion.43, f32[64,512,64]{1,0,2:T(8,128)} %fusion.63, ...), kind=kOutput, calls=%fused_computation.72 | convolution fusion | flops 1656811520 | bytes 150994944 | tf_op jit(solution)/shard_map/rkb,bm->rmk/dot_general | solution.py:19
  2801.2 19.4 subtract_bitcast_fusion.1
  2820.6 18.0 fusion.35
  2851.4 15.6 subtract_bitcast_fusion
  2878.6 14.0 add_bitcast_fusion
  2901.0 36.9 %fusion.9 = (f32[512,8,512]{0,2,1:T(8,128)}, f32[512,8,512]{0,2,1:T(8,128)S(1)}) fusion(s32[8,512]{1,0:T(8,128)S(1)} %copy-done.24, s32[512]{0:T(512)S(1)} %copy-done.26, f32[512,8,512]{0,2,1:T(8,128)S(1)} %bitcast.487, f32[512,8,512]{0,2,1:T(8,128)S(1)} %bitcast.486), kind=kLoop, calls=%fused_computation.28 | loop fusion | flops 41943040 | bytes 33572864 | tf_op jit(solution)/shard_map/add | solution.py:31
  2937.9 186.7 %all_to_all.61 = f32[512,8,512]{0,2,1:T(8,128)} all-to-all(f32[512,8,512]{0,2,1:T(8,128)S(1)} %get-tuple-element.36), channel_id=1, replica_groups=mesh['entry'=4,'fft'=8] {'fft'}, dimensions={1} | all-to-all | bytes 16777216 | tf_op jit(solution)/shard_map/all_to_all | solution.py:202
  3169.9 141.7 %all-to-all-done.4 = f32[512,8,512]{0,2,1:T(8,128)} async-done(((f32[512,8,512]{0,2,1:T(8,128)}), f32[512,8,512]{0,2,1:T(8,128)}, u32[]{:S(2)}, u32[]{:S(2)}) %all-to-all-start.4) | async-done | bytes 8388640 | tf_op jit(solution)/shard_map/all_to_all | solution.py:203
  3358.6 16.6 fusion.26
  (243 shorter events, 758.6 us)
Async XLA Ops:
  13.1 190.7 %all-to-all-start = ((f32[4,4,512,512]{3,2,0,1:T(8,128)}), f32[4,4,512,512]{3,2,0,1:T(8,128)}, u32[]{:S(2)}, u32[]{:S(2)}) async-start(f32[4,4,512,512]{3,2,0,1:T(8,128)} %pad_maximum_fusion.2), calls=%async_computation | async-start | bytes 33554432 | tf_op jit(solution)/shard_map/all_to_all | solution.py:153
  20.4 287.1 %copy-start.19 = (f32[64,64]{0,1:T(8,128)}, f32[64,64]{0,1:T(8,128)S(1)}, u32[]{:S(2)}) copy-start(f32[64,64]{0,1:T(8,128)S(1)} %copy.348) | copy-start | bytes 49156
  20.7 286.8 %copy-start.21 = (f32[64,64]{0,1:T(8,128)}, f32[64,64]{0,1:T(8,128)S(1)}, u32[]{:S(2)}) copy-start(f32[64,64]{0,1:T(8,128)S(1)} %copy.350) | copy-start | bytes 49156
  353.0 18.2 copy-start.3
  353.0 31.7 slice-start.26
  371.2 13.5 slice-start.27
  384.7 26.6 slice-start.24
  411.2 26.9 slice-start.22
  424.5 13.6 slice-start.23
  438.1 26.7 slice-start.6
  438.1 26.7 slice-start.40
  478.6 39.4 %slice-start.4 = ((s8[8388608]{0:T(1024)(128)(4,1)}), s8[4194304]{0:T(1024)(128)(4,1)S(1)}, s32[]{:S(2)}) async-start(s8[8388608]{0:T(1024)(128)(4,1)} %bitcast.413), calls=%async_computation.9 | async-start | bytes 8388608
  490.4 27.7 slice-start.5
  533.2 35.4 %slice-start.2 = ((s8[8388608]{0:T(1024)(128)(4,1)}), s8[4194304]{0:T(1024)(128)(4,1)S(1)}, s32[]{:S(2)}) async-start(s8[8388608]{0:T(1024)(128)(4,1)} %bitcast.411), calls=%async_computation.7 | async-start | bytes 8388608
  541.3 27.3 slice-start.3
  584.6 39.0 %slice-start = ((s8[8388608]{0:T(1024)(128)(4,1)}), s8[4194304]{0:T(1024)(128)(4,1)S(1)}, s32[]{:S(2)}) async-start(s8[8388608]{0:T(1024)(128)(4,1)} %bitcast.409), calls=%async_computation.5 | async-start | bytes 8388608
  596.3 27.3 slice-start.1
  638.8 35.8 %slice-start.38 = ((s8[8388608]{0:T(1024)(128)(4,1)}), s8[4194304]{0:T(1024)(128)(4,1)S(1)}, s32[]{:S(2)}) async-start(s8[8388608]{0:T(1024)(128)(4,1)} %bitcast.471), calls=%async_computation.43 | async-start | bytes 8388608
  647.0 27.6 slice-start.39
  781.6 732.0 %all-to-all-start.2 = ((f32[4,4096,512]{2,0,1:T(4,128)}), f32[4,4096,512]{2,0,1:T(4,128)}, u32[]{:S(2)}, u32[]{:S(2)}) async-start(f32[4,4096,512]{2,0,1:T(4,128)} %copy.386), calls=%async_computation.2 | async-start | bytes 67108864 | tf_op jit(solution)/shard_map/all_to_all | solution.py:177
  1513.6 729.0 %all-to-all-start.1 = ((f32[4,4096,512]{2,0,1:T(4,128)}), f32[4,4096,512]{2,0,1:T(4,128)}, u32[]{:S(2)}, u32[]{:S(2)}) async-start(f32[4,4096,512]{2,0,1:T(4,128)} %copy.381), calls=%async_computation.1 | async-start | bytes 67108864 | tf_op jit(solution)/shard_map/all_to_all | solution.py:174
  1613.5 36.1 %slice-start.36 = ((s8[8388608]{0:T(1024)(128)(4,1)}), s8[4194304]{0:T(1024)(128)(4,1)S(1)}, s32[]{:S(2)}) async-start(s8[8388608]{0:T(1024)(128)(4,1)} %bitcast.451), calls=%async_computation.41 | async-start | bytes 8388608
  1631.5 18.1 slice-start.37
  1649.6 27.2 slice-start.32
  1676.8 26.8 slice-start.34
  2307.0 17.9 copy-start.4
  2347.4 18.0 copy-start.5
  2388.1 18.0 copy-start.6
  2429.1 17.8 copy-start.20
  2429.1 17.8 copy-start.22
  2511.2 18.1 copy-start.1
  2511.2 31.8 slice-start.20
  2529.2 13.8 slice-start.21
  2543.0 26.9 slice-start.18
  2556.4 13.5 slice-start.19
  2569.9 26.7 slice-start.16
  2583.1 13.5 slice-start.17
  2596.6 27.0 slice-start.14
  2609.9 13.7 slice-start.15
  2623.7 26.8 slice-start.12
  2650.4 26.9 slice-start.10
  2677.3 27.1 slice-start.8
  2690.7 13.7 slice-start.9
  2769.0 22.3 slice-start.30
  2820.6 18.0 copy-start.8
  2820.6 30.8 slice-start.28
  3124.6 187.0 %all-to-all-start.4 = ((f32[512,8,512]{0,2,1:T(8,128)}), f32[512,8,512]{0,2,1:T(8,128)}, u32[]{:S(2)}, u32[]{:S(2)}) async-start(f32[512,8,512]{0,2,1:T(8,128)} %get-tuple-element.35), calls=%async_computation.4 | async-start | bytes 16777216 | tf_op jit(solution)/shard_map/all_to_all | solution.py:203
  3358.6 16.7 copy-start.13
  (25 other events, 260.2 us)
where the time goes:
time: 3410 us; the launch traced here: 3400 us
  waiting for transfers between devices  1500 us (44%)
  matrix products  1090 us (32%)
  local copies, waits for them, and re-layouts  444 us (13%)
  blocking collectives  187 us (5%)
  other arithmetic  150 us (4%)
    dot_general x58, matrix products, contract(): jnp.einsum(pattern, left_op, right_op, precision=exact_precision, preferr...  928 us
    all_to_all x1, waiting for transfers between devices, local(): lax.all_to_all(jnp.stack(imag_list), 'fft', split_axis=1, concat_axis=2,...  664 us
    all_to_all x1, waiting for transfers between devices, local(): lax.all_to_all(jnp.stack(real_list), 'fft', split_axis=1, concat_axis=2,...  512 us
    all_to_all x1, blocking collectives, local(): lax.all_to_all(mixed_real, 'fft', split_axis=1, concat_axis=0, tiled=True)  187 us
    all_to_all x1, waiting for transfers between devices, local(): lax.all_to_all(outgoing, 'entry', split_axis=1, concat_axis=1, tiled=True)  183 us
    dot_general x12, matrix products, matmul(): jnp.dot(left_op, right_op, precision=exact_precision, preferred_element_t...  160 us
    all_to_all x1, waiting for transfers between devices, local(): lax.all_to_all(mixed_imag, 'fft', split_axis=1, concat_axis=0, tiled=True)  142 us
    add x2, other arithmetic, rotate(): real_part * sine + imag_part * cosine  82.9 us
  transfers between devices with their start and end apart: 4, of which 4 were waited for; matrix products, arithmetic and copies ran while one was open for 9% of the time, Pallas kernels for 0%

commit v1 on v0

v1 whole, which is shorter than its diff:
```python
import math

import jax
import jax.numpy as jnp
import numpy as np
from jax import lax
from jax.sharding import PartitionSpec as P

LANES = 128
BOTH = ("entry", "fft")
three_pass = lax.Precision.HIGH


def contract(pattern, left_op, right_op):
    return jnp.einsum(
        pattern, left_op, right_op, precision=three_pass, preferred_element_type=jnp.float32
    )


def digits(limbs):
    return (limbs.astype(jnp.float32) - 32768.0) * (1.0 / 32768.0)


def column_tables(half, devices):
    rows = half // (2 * devices)
    length = 2 * half
    freq = 2 * np.arange(devices * rows, dtype=np.int64)[None] + np.arange(2)[:, None]
    freq = freq.reshape(2, devices, 1, rows, 1)
    place = np.arange(half, dtype=np.int64)
    turns = freq * place % length
    wave = np.concatenate(
        [np.cos(turns * (2 * np.pi / length)), -np.sin(turns * (2 * np.pi / length))], axis=2
    )
    wave[0, 0, 1, 0] = 1.0 - 2.0 * (place % 2)
    return wave.astype(np.float32).reshape(2, half, half)


def complex_table(count, sign):
    index = np.arange(count)
    angle = (index[:, None] * index[None] % count) * (2 * np.pi / count)
    cosine, sine = np.cos(angle), sign * np.sin(angle)
    return np.stack(
        [np.stack([cosine, sine], axis=1), np.stack([-sine, cosine], axis=1)]
    ).astype(np.float32)


def rotate(real_part, imag_part, cosine, sine):
    return (real_part * cosine - imag_part * sine, real_part * sine + imag_part * cosine)


def local(a00, a01, a10, a11, b00, b01, b10, b11):
    devices = lax.axis_size("entry") * lax.axis_size("fft")
    entries = lax.axis_size("entry")
    groups = lax.axis_size("fft")
    cols = a00.shape[1]
    half = a00.shape[0] * entries
    columns = cols * groups
    length = 2 * half * columns
    rows = half // (2 * devices)
    lanes = min(LANES, cols)
    inner = cols // lanes
    outer = groups * inner
    mine = lax.axis_index("entry") * groups + lax.axis_index("fft")
    first = mine == 0

    heads = jnp.stack([digits(x) for x in (a00, a10, b00, b01)])
    tails = jnp.stack([digits(x) for x in (a01, a11, b10, b11)])
    outgoing = jnp.concatenate([heads, tails], axis=2)
    arrived = lax.all_to_all(outgoing, "entry", split_axis=0, concat_axis=0, tiled=True)
    sequence = arrived.reshape(half, 2 * cols)

    waves = column_tables(half, devices)
    outer_ahead = complex_table(outer, -1.0).reshape(2, groups, inner, 2, outer)
    outer_back = complex_table(outer, 1.0).reshape(2, outer, 2, groups, inner)
    lane_ahead = complex_table(lanes, -1.0)
    lane_back = complex_table(lanes, 1.0)
    turn = np.arange(outer)[:, None] * np.arange(lanes)[None] * (2 * np.pi / columns)
    turn_cos = np.cos(turn).astype(np.float32)[:, None, :]
    turn_sin = np.sin(turn).astype(np.float32)[:, None, :]

    pieces = []
    for parity in range(2):
        sent = contract("sp,pq->sq", waves[parity], sequence)
        sent = sent.reshape(devices, 2 * rows, 2 * cols)
        pieces.append(lax.all_to_all(sent, BOTH, split_axis=0, concat_axis=0, tiled=True))

    results = []
    for parity in range(2):
        piece = pieces[parity].reshape(entries, groups, 2, rows, 2, inner, lanes)
        real_part, imag_part = piece[:, :, 0], piece[:, :, 1]
        freq = 2 * (mine * rows + jnp.arange(rows, dtype=jnp.int32)) + parity
        if parity == 0:
            lead = first & (jnp.arange(rows) == 0)
            lead = lead[:, None, None, None]
            extra = imag_part[:, :, :1]
            imag_part = jnp.where(lead, 0.0, imag_part)
            real_part = jnp.concatenate([real_part, extra], axis=2)
            imag_part = jnp.concatenate([imag_part, jnp.zeros_like(extra)], axis=2)
            freq = jnp.concatenate([freq, jnp.full((1,), half, jnp.int32)])
        place = jnp.arange(columns, dtype=jnp.int32).reshape(groups, 1, inner, lanes)
        angle = (freq[:, None, None] * place % length).astype(jnp.float32)
        angle = angle * (2.0 * math.pi / length)
        cosine, sine = jnp.cos(angle), jnp.sin(angle)
        real_part, imag_part = rotate(
            real_part, imag_part, cosine[:, :, None], -sine[:, :, None]
        )
        both = jnp.stack([real_part, imag_part])
        step = contract("pefrnab,pfaqc->qnecrb", both, outer_ahead)
        step = jnp.stack(rotate(step[0], step[1], turn_cos, -turn_sin))
        spec = contract("pnecrb,pbqm->qnecrm", step, lane_ahead)
        left_real, left_imag = spec[0, :, :2, None], spec[1, :, :2, None]
        right_real, right_imag = spec[0, :, None, 2:], spec[1, :, None, 2:]
        mixed_real = jnp.sum(left_real * right_real - left_imag * right_imag, axis=0)
        mixed_imag = jnp.sum(left_real * right_imag + left_imag * right_real, axis=0)
        mixed = jnp.stack([mixed_real, mixed_imag])
        mixed = mixed.reshape((2, 4) + mixed.shape[3:])
        step = contract("pncrm,pmqb->qncrb", mixed, lane_back)
        step = jnp.stack(rotate(step[0], step[1], turn_cos, turn_sin))
        back = contract("pncrb,pcqfa->qnfrab", step, outer_back)
        scale = 2.0 / (length * math.sqrt(length // 2))
        back_real, back_imag = rotate(back[0], back[1], cosine * scale, sine * scale)
        if parity == 0:
            extra = back_real[:, :, rows:]
            back_real = back_real[:, :, :rows]
            back_imag = back_imag[:, :, :rows]
            back_lead = lead[:, 0]
            back_imag = jnp.where(back_lead, 0.5 * extra, back_imag)
            back_real = jnp.where(back_lead, 0.5 * back_real, back_real)
        home = jnp.stack([back_real, back_imag], axis=2)
        home = home.reshape(devices, 2 * rows, cols)
        home = lax.all_to_all(home, BOTH, split_axis=0, concat_axis=0, tiled=True)
        results.append(contract("sp,sq->pq", waves[parity], home.reshape(half, cols)))
    even, odd = results
    return jnp.stack([even + odd, even - odd]).reshape(1, 2 * half, cols)


def solution(mesh):
    return jax.shard_map(
        local,
        mesh=mesh,
        in_specs=(P("entry", "fft"),) * 8,
        out_specs=P("entry", None, "fft"),
        check_vma=False,
    )
```

time: 3410 us -> 759 us (0.22)
  waiting for transfers between devices: 1500 us -> 361 us
  matrix products: 1090 us -> 147 us
  local copies, waits for them, and re-layouts: 444 us -> 79.1 us
  other arithmetic: 150 us -> 45.8 us
  blocking collectives: 187 us -> 97.1 us
    all_to_all x4, waiting for transfers between devices: 1500 us -> 361 us  [the longest x2 259 us: local(): lax.all_to_all(sent, BOTH, split_axis=0, concat_axis=0, tiled=True)]
    dot_general x70 -> x12, matrix products: 1090 us -> 147 us  [contract(): jnp.einsum(pattern, left_op, right_op, precision=three_pass, preferred_el...]
    slice x11 -> x5, local copies, waits for them, and re-layouts: 134 us -> 11.6 us  [the longest x2 9.84 us: local(): real_part, imag_part = (piece[:, :, 0], piece[:, :, 1])]
    all_to_all x1, blocking collectives: 187 us -> 97.1 us  [local(): lax.all_to_all(outgoing, 'entry', split_axis=0, concat_axis=0, tiled=True)]
    add x3 -> x0, other arithmetic: 83.5 us -> none  [the longest x2 82.9 us: rotate(): real_part * sine + imag_part * cosine]
    another operation x6 -> x3, local copies, waits for them, and re-layouts: 95.7 us -> 15.3 us  [the longest x1 8.67 us: local(): return jnp.stack([even + odd, even - odd]).reshape(1, 2 * half, cols)]
    all_to_all x4 -> x0, local copies, waits for them, and re-layouts: 79.8 us -> none  [the longest x1 31 us: local(): lax.all_to_all(jnp.stack(real_list), 'fft', split_axis=1, concat_axis=2,...]
    add x5 -> x0, local copies, waits for them, and re-layouts: 54.8 us -> none  [the longest x4 46.4 us: column_transform(): contract('mb,kbc->mkc', second_sin, step_real)]
  transfers between devices with their start and end apart: 4 -> 4, of which waited for: 4 -> 4; matrix products, arithmetic and copies ran while one was open for 9% -> 26% of each run, Pallas kernels for 0% -> 0%
where the time goes in v1:
time: 759 us; the launch traced here: 752 us
  waiting for transfers between devices  361 us (48%)
  matrix products  147 us (19%)
  blocking collectives  97.1 us (13%)
  local copies, waits for them, and re-layouts  79.1 us (10%)
  other arithmetic  45.8 us (6%)
  starting transfers between devices  20.7 us (3%)
    all_to_all x2, waiting for transfers between devices, local(): lax.all_to_all(sent, BOTH, split_axis=0, concat_axis=0, tiled=True)  259 us
    dot_general x12, matrix products, contract(): jnp.einsum(pattern, left_op, right_op, precision=three_pass, preferred_el...  147 us
    all_to_all x2, waiting for transfers between devices, local(): home = lax.all_to_all(home, BOTH, split_axis=0, concat_axis=0, tiled=True)  102 us
    all_to_all x1, blocking collectives, local(): lax.all_to_all(outgoing, 'entry', split_axis=0, concat_axis=0, tiled=True)  97.1 us
    reshape x2, local copies, waits for them, and re-layouts, local(): piece = pieces[parity].reshape(entries, groups, 2, rows, 2, inner, lanes)  21.4 us
    sub x7, other arithmetic, rotate(): real_part * cosine - imag_part * sine  15.4 us
  transfers between devices with their start and end apart: 4, of which 4 were waited for; matrix products, arithmetic and copies ran while one was open for 26% of the time, Pallas kernels for 0%

profile of v1, /device:TPU:0, one launch (start us, length us, event | category | flops | bytes accessed | tf_op | source)
XLA Modules:
  0.0 751.9 jit_solution(1252208097911665105)
XLA Ops:
  0.0 2.0 multiply_bitcast_fusion
  5.0 97.1 %all_to_all.25 = f32[4,512,1024]{2,1,0:T(8,128)S(1)} all-to-all(f32[4,512,1024]{2,1,0:T(8,128)S(1)} %maximum_maximum_fusion), channel_id=1, replica_groups=mesh['entry'=4,'fft'=8] {'entry'}, dimensions={0} | all-to-all | bytes 16777216 | tf_op jit(solution)/shard_map/all_to_all | solution.py:69
  102.1 36.1 %fusion.59 = f32[2048,1024]{1,0:T(8,128)} fusion(f32[2048,2048]{1,0:T(8,128)} %constant.95.clone, f32[2048,1024]{1,0:T(8,128)S(1)} %bitcast.216), kind=kOutput, calls=%fused_computation.133 | convolution fusion | flops 25769803776 | bytes 33554432 | tf_op jit(solution)/shard_map/sp,pq->sq/dot_general | solution.py:15
  138.2 5.4 all-to-all-start.1
  143.6 33.5 %fusion.61 = f32[2048,1024]{1,0:T(8,128)} fusion(f32[2048,2048]{1,0:T(8,128)} %constant.96.clone, f32[2048,1024]{1,0:T(8,128)} %bitcast.217), kind=kOutput, calls=%fused_computation.135 | convolution fusion | flops 25769803776 | bytes 33554432 | tf_op jit(solution)/shard_map/sp,pq->sq/dot_general | solution.py:15
  177.1 152.3 %all-to-all-done.1 = f32[32,64,1024]{2,1,0:T(8,128)} async-done(((f32[32,64,1024]{2,1,0:T(8,128)}), f32[32,64,1024]{2,1,0:T(8,128)}, u32[]{:S(2)}, u32[]{:S(2)}) %all-to-all-start.1) | async-done | bytes 8388640 | tf_op jit(solution)/shard_map/all_to_all | solution.py:85
  329.4 5.8 all-to-all-start.3
  335.3 2.2 broadcast_multiply_fusion
  339.4 10.9 %reshape.268 = f32[4,8,2,32,2,4,128]{6,5,4,3,2,1,0:T(4,128)} reshape(f32[32,64,1024]{2,1,0:T(8,128)} %all-to-all-done.1) | data formatting | bytes 16777216 | tf_op jit(solution)/shard_map/reshape | solution.py:89
  350.3 4.9 fusion.58
  355.2 2.4 copy.132
  357.6 2.4 copy.133
  360.1 2.8 broadcast_select_fusion
  362.9 1.6 subtract_bitcast_fusion
  364.5 4.0 fusion.23
  368.6 1.6 multiply_subtract_fusion
  370.2 1.5 maximum_bitcast_fusion.2
  371.7 10.6 %fusion.20 = f32[2,2,4,32,33,128]{5,4,0,3,2,1:T(8,128)S(1)} fusion(f32[2,128,2,128,1,1,1]{3,1,0,2,6,5,4:T(8,128)S(1)} %copy-done.7, f32[2,2,4,32,33,128,1]{5,3,0,1,4,2,6:T(8,128)S(1)} %maximum_bitcast_fusion.2), kind=kOutput, calls=%fused_computation.51 | convolution fusion | flops 3321888768 | bytes 17563648 | tf_op jit(solution)/shard_map/pnecrb,pbqm->qnecrm/dot_general | solution.py:15
  382.3 3.4 slice_bitcast_fusion.3
  385.7 2.3 copy.52
  389.8 2.4 subtract_reduce_fusion
  394.8 2.3 fusion.28
  398.5 3.2 fusion.29
  405.4 3.4 copy.60
  408.8 5.5 reshape.275
  414.3 106.7 %all-to-all-done.3 = f32[32,64,1024]{2,1,0:T(8,128)} async-done(((f32[32,64,1024]{2,1,0:T(8,128)}), f32[32,64,1024]{2,1,0:T(8,128)}, u32[]{:S(2)}, u32[]{:S(2)}) %all-to-all-start.3) | async-done | bytes 8388640 | tf_op jit(solution)/shard_map/all_to_all | solution.py:85
  521.0 5.8 all-to-all-start.2
  526.8 3.2 broadcast_multiply_fusion.3
  529.9 10.5 %reshape.278 = f32[4,8,2,32,2,4,128]{6,5,4,3,2,1,0:T(4,128)} reshape(f32[32,64,1024]{2,1,0:T(8,128)} %all-to-all-done.3) | data formatting | bytes 16777216 | tf_op jit(solution)/shard_map/reshape | solution.py:89
  540.5 4.9 fusion.57
  545.4 8.2 %multiply_subtract_fusion.2 = (f32[1,4,8,32,2,4,128]{6,2,0,5,4,3,1:T(8,128)S(1)}, f32[1,4,8,32,2,4,128]{6,2,0,5,4,3,1:T(8,128)}) fusion(f32[4,8,1,32,2,4,128]{6,5,4,3,2,1,0:T(4,128)S(1)} %get-tuple-element.28, f32[4,8,1,32,2,4,128]{6,5,4,3,2,1,0:T(4,128)S(1)} %get-tuple-element.27, f32[8,32,4,128]{3,0,2,1:T(8,128)S(1)} %get-tuple-element.41, ...), kind=kLoop, calls=%fused_computation.50 | loop fusion | flops 6291456 | bytes 17825792 | tf_op jit(solution)/shard_map/sub | solution.py:48
  553.6 6.1 fusion.27
  559.6 3.1 multiply_subtract_fusion.1
  562.7 3.7 maximum_bitcast_fusion.5
  566.4 9.0 %fusion.24 = f32[2,2,4,32,32,128]{5,4,0,3,2,1:T(8,128)S(1)} fusion(f32[2,128,2,128,1,1,1]{3,1,0,2,6,5,4:T(8,128)S(1)} %copy-done.8, f32[2,2,4,32,32,128,1]{5,3,0,1,4,2,6:T(8,128)S(1)} %maximum_bitcast_fusion.5), kind=kOutput, calls=%fused_computation.53 | convolution fusion | flops 3221225472 | bytes 17039360 | tf_op jit(solution)/shard_map/pnecrb,pbqm->qnecrm/dot_general | solution.py:15
  575.4 1.4 slice_bitcast_fusion.11
  576.8 2.1 subtract_reduce_fusion.1
  578.9 1.8 fusion.35
  582.1 4.4 fusion.32
  587.6 3.3 copy.66
  590.9 5.5 reshape.279
  596.3 25.6 %all-to-all-done.2 = f32[32,64,512]{2,1,0:T(8,128)} async-done(((f32[32,64,512]{2,1,0:T(8,128)}), f32[32,64,512]{2,1,0:T(8,128)}, u32[]{:S(2)}, u32[]{:S(2)}) %all-to-all-start.2) | async-done | bytes 4194336 | tf_op jit(solution)/shard_map/all_to_all | solution.py:131
  621.9 3.8 all-to-all-start.4
  625.7 18.4 %fusion.60 = f32[512,2048]{1,0:T(8,128)} fusion(f32[2048,512]{1,0:T(8,128)} %bitcast.57, f32[2048,2048]{1,0:T(8,128)} %constant.95.clone), kind=kOutput, calls=%fused_computation.134 | convolution fusion | flops 12884901888 | bytes 25165824 | tf_op jit(solution)/shard_map/sp,sq->pq/dot_general | solution.py:15
  644.1 76.7 %all-to-all-done.4 = f32[32,64,512]{2,1,0:T(8,128)} async-done(((f32[32,64,512]{2,1,0:T(8,128)}), f32[32,64,512]{2,1,0:T(8,128)}, u32[]{:S(2)}, u32[]{:S(2)}) %all-to-all-start.4) | async-done | bytes 4194336 | tf_op jit(solution)/shard_map/all_to_all | solution.py:131
  720.8 17.8 %add_bitcast_fusion.1 = (f32[1,2048,512]{1,2,0:T(8,128)S(1)}, f32[1,2048,512]{1,2,0:T(8,128)S(1)}) fusion(f32[512,2048]{1,0:T(8,128)} %fusion.60, f32[2048,512]{1,0:T(8,128)} %bitcast.96, f32[2048,2048]{1,0:T(8,128)} %constant.96.clone), kind=kOutput, calls=%fused_computation.44 | convolution fusion | flops 12886999040 | bytes 33554432 | tf_op jit(solution)/shard_map/sp,sq->pq/dot_general | solution.py:15
  738.7 4.3 pad_maximum_fusion
  743.0 8.7 %copy.67 = f32[2,2048,512]{2,1,0:T(8,128)} copy(f32[2,2048,512]{1,2,0:T(8,128)} %pad_maximum_fusion) | data formatting | bytes 16777216 | tf_op jit(solution)/shard_map/stack | solution.py:134
  (77 shorter events, 16.7 us)
Async XLA Ops:
  0.0 2.0 copy-start.10
  0.0 2.2 copy-start.9
  0.0 2.5 copy-start.12
  0.0 2.8 copy-start.11
  2.2 1.4 copy-start.13
  2.2 1.7 copy-start.14
  102.1 36.1 %copy-start.2 = (f32[4,512,1024]{2,1,0:T(8,128)}, f32[4,512,1024]{2,1,0:T(8,128)S(1)}, u32[]{:S(2)}) copy-start(f32[4,512,1024]{2,1,0:T(8,128)S(1)} %all_to_all.25) | copy-start | bytes 25165828
  138.2 191.2 %all-to-all-start.1 = ((f32[32,64,1024]{2,1,0:T(8,128)}), f32[32,64,1024]{2,1,0:T(8,128)}, u32[]{:S(2)}, u32[]{:S(2)}) async-start(f32[32,64,1024]{2,1,0:T(8,128)} %bitcast.218), calls=%async_computation.1 | async-start | bytes 16777216 | tf_op jit(solution)/shard_map/all_to_all | solution.py:85
  329.4 191.6 %all-to-all-start.3 = ((f32[32,64,1024]{2,1,0:T(8,128)}), f32[32,64,1024]{2,1,0:T(8,128)}, u32[]{:S(2)}, u32[]{:S(2)}) async-start(f32[32,64,1024]{2,1,0:T(8,128)} %bitcast.215), calls=%async_computation.3 | async-start | bytes 16777216 | tf_op jit(solution)/shard_map/all_to_all | solution.py:85
  337.5 1.0 copy-start.3
  362.9 1.6 copy-start.19
  364.5 4.0 copy-start.21
  364.5 4.0 copy-start.23
  370.2 1.5 copy-start.7
  385.7 2.5 copy-start.1
  385.7 3.3 copy-start
  392.2 2.6 copy-start.15
  394.8 2.3 copy-start.22
  397.7 0.8 copy-start.17
  398.5 3.2 copy-start.4
  402.5 1.0 copy-start.5
  402.5 1.2 copy-start.6
  521.0 100.9 %all-to-all-start.2 = ((f32[32,64,512]{2,1,0:T(8,128)}), f32[32,64,512]{2,1,0:T(8,128)}, u32[]{:S(2)}, u32[]{:S(2)}) async-start(f32[32,64,512]{2,1,0:T(8,128)} %reshape.275), calls=%async_computation.2 | async-start | bytes 8388608 | tf_op jit(solution)/shard_map/all_to_all | solution.py:131
  545.4 8.2 %copy-start.20 = (f32[2,8,4,2,32,1,1,1]{4,1,0,2,3,7,6,5:T(8,128)S(1)}, f32[2,8,4,2,32,1,1,1]{4,1,0,2,3,7,6,5:T(8,128)}, u32[]{:S(2)}) copy-start(f32[2,8,4,2,32,1,1,1]{4,1,0,2,3,7,6,5:T(8,128)} %constant.109) | copy-start | bytes 49156
  553.6 6.1 copy-start.24
  562.7 3.7 copy-start.8
  576.8 2.1 copy-start.16
  581.3 0.8 copy-start.18
  621.9 98.9 %all-to-all-start.4 = ((f32[32,64,512]{2,1,0:T(8,128)}), f32[32,64,512]{2,1,0:T(8,128)}, u32[]{:S(2)}, u32[]{:S(2)}) async-start(f32[32,64,512]{2,1,0:T(8,128)} %reshape.279), calls=%async_computation.4 | async-start | bytes 8388608 | tf_op jit(solution)/shard_map/all_to_all | solution.py:131
